TPU v7x, 32 devices: a whole 2x2x4 slice. The times are simulated.
32 devices in a mesh: occ: 2 (over x), vir: 16 (over z, y, core).
Axes of the slice: x: 2, y: 2, z: 4, core: 2. Of those that a mesh axis runs over, the one named last changes fastest.
Arguments:
- amplitudes: bfloat16 [256, 240, 2112], P(('occ', 'vir')), may hold values from -6 to 6
- integrals: bfloat16 [240, 2112, 256], P('occ', 'vir'), may hold values from -0.01171875 to 0.01171875
- screen: int32 [5, 22], replicated, may hold values 0 or 1
- row_gap: float32 [256], P('occ'), may hold values from 0.2 to 2
- col_gap: float32 [256], P('vir'), may hold values from 0.2 to 2
Outputs:
- update: float32 [256, 256], P('occ', 'vir')
Inputs may be any that keep to these rules, and one draw needn't show every extreme that they name: `screen`: 1 keeps the amplitudes of an occupied tile and a virtual tile, 0 screens them out.
All inputs are finite; a program needn't handle non-finite values.
Results may differ from a plain program's by a relative error of at most 0.0003.
Values may be sent and summed in bfloat16 or wider, within the bound.
A program may use at most 128 MiB of HBM per device.

v0:
```python
import jax
import jax.numpy as jnp
from jax import lax
from jax.sharding import PartitionSpec as P


def shards(amplitudes, integrals, screen, row_gap, col_gap):
    rows_here, occ_all, vir_all = amplitudes.shape
    tiles_occ, tiles_vir = screen.shape
    keep_mask = jnp.broadcast_to(
        screen.astype(jnp.bfloat16)[:, None, :, None],
        (tiles_occ, occ_all // tiles_occ, tiles_vir, vir_all // tiles_vir),
    ).reshape(occ_all, vir_all)
    screened = amplitudes * keep_mask[None]
    occ_part, vir_part, col_total = integrals.shape
    relaid = lax.all_to_all(
        lax.all_to_all(screened[None, None], "occ", split_axis=3, concat_axis=0, tiled=True),
        "vir",
        split_axis=4,
        concat_axis=1,
        tiled=True,
    )
    flat_rows = relaid.reshape(-1, occ_part * vir_part)
    int_slab = integrals.reshape(occ_part * vir_part, col_total)
    per_vir = lax.psum_scatter(
        lax.dot_general(
            int_slab, flat_rows, (((0,), (1,)), ((), ())), preferred_element_type=jnp.float32
        ),
        "vir",
        scatter_dimension=0,
        tiled=True,
    )
    cycle_cols = lax.psum_scatter(per_vir, "occ", scatter_dimension=1, tiled=True)
    cycle_sum = cycle_cols.T
    update = cycle_sum / (row_gap[:, None] + col_gap[None, :])
    return update


def solution(mesh):
    placed = (P(("occ", "vir"), None, None), P("occ", "vir", None), P(), P("occ"), P("vir"))
    return jax.shard_map(
        shards, mesh=mesh, in_specs=placed, out_specs=P("occ", "vir"), check_vma=False
    )
```

profile of v0, /device:TPU:0, one launch (start us, length us, event | category | flops | bytes accessed | tf_op | source)
XLA Modules:
  0.0 464.6 jit_solution(2814639098561962855)
XLA Ops:
  6.5 0.7 convert_element_type.3
  7.2 0.3 broadcast_in_dim.4
  7.5 1.0 mul.10
  8.5 7.6 %fusion = bf16[1,1,8,240,2112]{4,2,1,0,3:T(8,128)(2,1)S(1)} fusion(bf16[8,240,2112]{2,1,0:T(8,128)(2,1)} %param.5, bf16[240,2112]{1,0:T(8,128)(2,1)S(1)} %mul.10), kind=kLoop, calls=%fused_computation.1 | loop fusion | flops 4055040 | bytes 17233920 | tf_op jit(solution)/shard_map/broadcast_in_dim | solution.py:17
  16.1 97.7 %all_to_all.33 = bf16[1,1,8,240,2112]{4,2,1,0,3:T(8,128)(2,1)} all-to-all(bf16[1,1,8,240,2112]{4,2,1,0,3:T(8,128)(2,1)S(1)} %fusion), channel_id=1, replica_groups=mesh['occ'=2,'vir'=16] {'occ'}, dimensions={3} | all-to-all | bytes 16220160 | tf_op jit(solution)/shard_map/all_to_all | solution.py:17
  113.9 7.6 %copy.22 = bf16[1,1,8,240,2112]{4,3,2,1,0:T(8,128)(2,1)} copy(bf16[1,1,8,240,2112]{4,2,1,0,3:T(8,128)(2,1)} %all_to_all.33) | data formatting | bytes 16220160 | tf_op jit(solution)/shard_map/all_to_all | solution.py:17
  121.5 22.5 %copy.23 = bf16[2,1,8,120,2112]{3,0,2,1,4:T(2,128)(2,1)} copy(bf16[2,1,8,120,2112]{4,3,0,2,1:T(8,128)(2,1)} %bitcast.22) | data formatting | bytes 16220160 | tf_op jit(solution)/shard_map/all_to_all | solution.py:17
  143.9 6.2 %all-to-all-start.1 = ((bf16[2,1,8,120,2112]{3,0,2,1,4:T(2,128)(2,1)}), bf16[2,1,8,120,2112]{3,0,2,1,4:T(2,128)(2,1)}, u32[]{:S(2)}, u32[]{:S(2)}) async-start(bf16[2,1,8,120,2112]{3,0,2,1,4:T(2,128)(2,1)} %copy.23), calls=%async_computation.1 | async-start | bytes 17301504 | tf_op jit(solution)/shard_map/all_to_all | solution.py:16
  150.2 0.0 reduce-scatter.7.cloned.1.call-start
  150.2 8.2 %copy.26 = bf16[120,132,256]{2,1,0:T(8,128)(2,1)} copy(bf16[120,132,256]{2,0,1:T(8,128)(2,1)} %param.6) | data formatting | bytes 16220160 | tf_op args[1]
  158.5 11.9 %reshape.12 = bf16[15840,256]{1,0:T(8,128)(2,1)} reshape(bf16[120,132,256]{2,1,0:T(8,128)(2,1)} %copy.26) | data formatting | bytes 16220160 | tf_op jit(solution)/shard_map/reshape | solution.py:24
  170.4 135.1 %all-to-all-done.1 = bf16[2,1,8,120,2112]{3,0,2,1,4:T(2,128)(2,1)} async-done(((bf16[2,1,8,120,2112]{3,0,2,1,4:T(2,128)(2,1)}), bf16[2,1,8,120,2112]{3,0,2,1,4:T(2,128)(2,1)}, u32[]{:S(2)}, u32[]{:S(2)}) %all-to-all-start.1) | async-done | bytes 8110112 | tf_op jit(solution)/shard_map/all_to_all | solution.py:16
  305.5 7.9 %copy.24 = bf16[2,1,8,120,2112]{3,2,4,0,1:T(8,128)(2,1)} copy(bf16[2,1,8,120,2112]{3,0,2,1,4:T(2,128)(2,1)} %all-to-all-done.1) | data formatting | bytes 16220160 | tf_op jit(solution)/shard_map/all_to_all | solution.py:16
  313.4 15.9 %copy.25 = bf16[2,16,1,8,120,132]{5,4,3,1,0,2:T(8,128)(2,1)} copy(bf16[2,16,1,8,120,132]{4,3,5,1,0,2:T(8,128)(2,1)} %bitcast.21) | data formatting | bytes 16220160 | tf_op jit(solution)/shard_map/all_to_all | solution.py:16
  329.2 20.0 %reshape.11 = bf16[256,15840]{1,0:T(8,128)(2,1)} reshape(bf16[2,16,1,8,120,132]{5,4,3,1,0,2:T(8,128)(2,1)} %copy.25) | data formatting | bytes 16220160 | tf_op jit(solution)/shard_map/reshape | solution.py:23
  349.2 7.9 %convolution_bitcast_fusion = f32[256,256]{0,1:T(8,128)S(1)} fusion(bf16[256,15840]{1,0:T(8,128)(2,1)} %reshape.11, bf16[15840,256]{1,0:T(8,128)(2,1)} %reshape.12), kind=kOutput, calls=%fused_computation.2 | convolution fusion | flops 2076180480 | bytes 16482304 | tf_op jit(solution)/shard_map/dot_general | solution.py:26
  357.1 0.8 copy.28
  357.9 0.0 reduce-scatter.7.cloned.1.call-update
  357.9 0.0 reduce-scatter.5.cloned.1.call-start
  358.0 87.3 %reduce-scatter.7.cloned.1.call-done = f32[16,256]{1,0:T(8,128)} async-done(((f32[256,256]{1,0:T(8,128)}), f32[16,256]{1,0:T(8,128)}) %reduce-scatter.7.cloned.1.call-update) | async-done | bytes 16400 | tf_op jit(solution)/shard_map/reduce_scatter | solution.py:25
  445.3 0.0 reduce-scatter.5.cloned.1.call-update
  445.3 11.0 %reduce-scatter.5.cloned.1.call-done = f32[16,128]{1,0:T(8,128)} async-done(((f32[16,256]{1,0:T(8,128)}), f32[16,128]{1,0:T(8,128)}) %reduce-scatter.5.cloned.1.call-update) | async-done | bytes 8208 | tf_op jit(solution)/shard_map/reduce_scatter | solution.py:33
  456.3 0.0 copy-done
  456.3 1.4 bitcast_divide_fusion
  (3 shorter events, 0.0 us)
Async XLA Ops:
  143.9 161.5 %all-to-all-start.1 = ((bf16[2,1,8,120,2112]{3,0,2,1,4:T(2,128)(2,1)}), bf16[2,1,8,120,2112]{3,0,2,1,4:T(2,128)(2,1)}, u32[]{:S(2)}, u32[]{:S(2)}) async-start(bf16[2,1,8,120,2112]{3,0,2,1,4:T(2,128)(2,1)} %copy.23), calls=%async_computation.1 | async-start | bytes 17301504 | tf_op jit(solution)/shard_map/all_to_all | solution.py:16
  150.2 295.1 %reduce-scatter.7.cloned.1.call-start = ((), (), s32[]{:S(2)}) async-start(), calls=%async_computation.5 | async-start | bytes 278528 | tf_op jit(solution)/shard_map/reduce_scatter | solution.py:25
  349.2 107.2 %copy-start = (f32[16]{0:T(128)S(1)}, f32[16]{0:T(128)}, u32[]{:S(2)}) copy-start(f32[16]{0:T(128)} %param.9) | copy-start | bytes 196
  349.2 107.2 %copy-start.1 = (f32[128]{0:T(128)S(1)}, f32[128]{0:T(128)}, u32[]{:S(2)}) copy-start(f32[128]{0:T(128)} %param.8) | copy-start | bytes 1540
  357.9 98.4 %reduce-scatter.5.cloned.1.call-start = ((), (), s32[]{:S(2)}) async-start(), calls=%async_computation.4 | async-start | bytes 24576 | tf_op jit(solution)/shard_map/reduce_scatter | solution.py:33
Sparse Core Ops, SparseCore 0:
  358.1 87.2 reduce-scatter.6
  447.5 8.7 reduce-scatter.4
where the time goes:
time: 467 us; the launch traced here: 465 us
  waiting for transfers between devices  233 us (50%)
  blocking collectives  97.7 us (21%)
  local copies, waits for them, and re-layouts  96.1 us (21%)
  between operations  13.5 us (3%)
  other arithmetic  9.62 us (2%)
  matrix products  7.89 us (2%)
  starting transfers between devices  6.32 us (1%)
    all_to_all x1, waiting for transfers between devices, shards(): lax.all_to_all(lax.all_to_all(screened[None, None], 'occ', split_axis=3,...  135 us
    all_to_all x1, blocking collectives, shards(): lax.all_to_all(screened[None, None], 'occ', split_axis=3, concat_axis=0,...  97.7 us
    reduce_scatter x1, waiting for transfers between devices, shards(): lax.psum_scatter(lax.dot_general(int_slab, flat_rows, (((0,), (1,)), ((),...  87.3 us
    all_to_all x2, local copies, waits for them, and re-layouts, shards(): lax.all_to_all(screened[None, None], 'occ', split_axis=3, concat_axis=0,...  30.1 us
    all_to_all x2, local copies, waits for them, and re-layouts, shards(): lax.all_to_all(lax.all_to_all(screened[None, None], 'occ', split_axis=3,...  23.7 us
    reshape x1, local copies, waits for them, and re-layouts, shards(): flat_rows = relaid.reshape(-1, occ_part * vir_part)  20 us
    reshape x1, local copies, waits for them, and re-layouts, shards(): int_slab = integrals.reshape(occ_part * vir_part, col_total)  11.9 us
    reduce_scatter x1, waiting for transfers between devices, shards(): lax.psum_scatter(per_vir, 'occ', scatter_dimension=1, tiled=True)  11 us
  transfers between devices with their start and end apart: 3, of which 3 were waited for; matrix products, arithmetic and copies ran while one was open for 4% of the time, Pallas kernels for 0%

commit v1 on v0

--- a/solution.py
+++ b/solution.py
@@ -14,7 +14,15 @@
     screened = amplitudes * keep_mask[None]
     occ_part, vir_part, col_total = integrals.shape
     relaid = lax.all_to_all(
-        lax.all_to_all(screened[None, None], "occ", split_axis=3, concat_axis=0, tiled=True),
+        jnp.concatenate(
+            lax.all_to_all(
+                jnp.stack(jnp.split(screened[None, None], lax.axis_size("occ"), axis=3)),
+                "occ",
+                0,
+                0,
+            ),
+            axis=0,
+        ),
         "vir",
         split_axis=4,
         concat_axis=1,

time: 467 us -> 466 us (level)
  local copies, waits for them, and re-layouts: 96.1 us -> 82.8 us
  blocking collectives: 97.7 us -> 104 us
  other arithmetic: 9.62 us -> 15.8 us
    all_to_all x4 -> x2, local copies, waits for them, and re-layouts: 53.8 us -> 23.1 us  [shards(): lax.all_to_all(jnp.concatenate(lax.all_to_all(jnp.stack(jnp.split(screene...]
    reshape x0 -> x1, local copies, waits for them, and re-layouts: none -> 12.5 us  [shards(): jnp.concatenate(lax.all_to_all(jnp.stack(jnp.split(screened[None, None],...]
    all_to_all x1, blocking collectives: 97.7 us -> 104 us  [shards(): lax.all_to_all(jnp.stack(jnp.split(screened[None, None], lax.axis_size('o...]
    another operation x0 -> x1, other arithmetic: none -> 6.28 us  [shards(): jnp.stack(jnp.split(screened[None, None], lax.axis_size('occ'), axis=3))]
    another operation x0 -> x1, local copies, waits for them, and re-layouts: none -> 5.05 us  [shards(): jnp.stack(jnp.split(screened[None, None], lax.axis_size('occ'), axis=3))]
where the time goes in v1:
time: 466 us; the launch traced here: 464 us
  waiting for transfers between devices  233 us (50%)
  blocking collectives  104 us (22%)
  local copies, waits for them, and re-layouts  82.8 us (18%)
  other arithmetic  15.8 us (3%)
  between operations  13.4 us (3%)
  matrix products  7.89 us (2%)
  starting transfers between devices  6.33 us (1%)
    all_to_all x1, waiting for transfers between devices, shards(): lax.all_to_all(jnp.concatenate(lax.all_to_all(jnp.stack(jnp.split(screene...  135 us
    all_to_all x1, blocking collectives, shards(): lax.all_to_all(jnp.stack(jnp.split(screened[None, None], lax.axis_size('o...  104 us
    reduce_scatter x1, waiting for transfers between devices, shards(): lax.psum_scatter(lax.dot_general(int_slab, flat_rows, (((0,), (1,)), ((),...  87.3 us
    all_to_all x2, local copies, waits for them, and re-layouts, shards(): lax.all_to_all(jnp.concatenate(lax.all_to_all(jnp.stack(jnp.split(screene...  23.1 us
    reshape x1, local copies, waits for them, and re-layouts, shards(): flat_rows = relaid.reshape(-1, occ_part * vir_part)  19.9 us
    reshape x1, local copies, waits for them, and re-layouts, shards(): jnp.concatenate(lax.all_to_all(jnp.stack(jnp.split(screened[None, None],...  12.5 us
    reshape x1, local copies, waits for them, and re-layouts, shards(): int_slab = integrals.reshape(occ_part * vir_part, col_total)  11.9 us
    reduce_scatter x1, waiting for transfers between devices, shards(): lax.psum_scatter(per_vir, 'occ', scatter_dimension=1, tiled=True)  11 us
  transfers between devices with their start and end apart: 3, of which 3 were waited for; matrix products, arithmetic and copies ran while one was open for 4% of the time, Pallas kernels for 0%

profile of v1, /device:TPU:0, one launch (start us, length us, event | category | flops | bytes accessed | tf_op | source)
XLA Modules:
  0.0 464.0 jit_solution(1362847301013523493)
XLA Ops:
  6.5 0.7 convert_element_type.3
  7.2 0.3 broadcast_in_dim.4
  7.5 1.0 mul.10
  8.5 7.5 %multiply_bitcast_fusion = bf16[1,1,8,240,2112]{4,3,2,1,0:T(8,128)(2,1)} fusion(bf16[8,240,2112]{2,1,0:T(8,128)(2,1)} %param.5, bf16[240,2112]{1,0:T(8,128)(2,1)S(1)} %mul.10), kind=kLoop, calls=%fused_computation.1 | loop fusion | flops 4055040 | bytes 17233920 | tf_op jit(solution)/shard_map/broadcast_in_dim | solution.py:19
  16.0 5.1 %slice_bitcast_fusion.1 = (bf16[1,1,1,8,120,2112]{5,4,3,2,1,0:T(8,128)(2,1)S(1)}, bf16[1,1,1,8,120,2112]{5,4,3,2,1,0:T(8,128)(2,1)}) fusion(bf16[1,1,8,240,2112]{4,3,2,1,0:T(8,128)(2,1)} %multiply_bitcast_fusion), kind=kLoop, calls=%fused_computation.3 | loop fusion | bytes 16220160 | tf_op jit(solution)/shard_map/stack | solution.py:19
  21.0 6.3 %pad_maximum_fusion = bf16[2,1,1,8,120,2112]{5,4,3,2,1,0:T(8,128)(2,1)} fusion(bf16[1,1,1,8,120,2112]{5,4,3,2,1,0:T(8,128)(2,1)} %get-tuple-element.6, bf16[1,1,1,8,120,2112]{5,4,3,2,1,0:T(8,128)(2,1)S(1)} %get-tuple-element.5), kind=kLoop, calls=%fused_computation | loop fusion | flops 4055040 | bytes 16220160 | tf_op jit(solution)/shard_map/stack | solution.py:19
  27.3 104.3 %all_to_all.20 = bf16[2,1,1,8,120,2112]{5,4,3,2,1,0:T(8,128)(2,1)} all-to-all(bf16[2,1,1,8,120,2112]{5,4,3,2,1,0:T(8,128)(2,1)} %pad_maximum_fusion), channel_id=1, replica_groups=mesh['occ'=2,'vir'=16] {'occ'}, dimensions={0} | all-to-all | bytes 16220160 | tf_op jit(solution)/shard_map/all_to_all | solution.py:18
  131.6 12.5 %copy.18 = bf16[2,1,8,120,2112]{3,2,0,1,4:T(8,128)(2,1)} copy(bf16[2,1,8,120,2112]{4,3,2,0,1:T(8,128)(2,1)} %bitcast.22) | data formatting | bytes 16220160 | tf_op jit(solution)/shard_map/reshape | solution.py:17
  144.1 6.2 %all-to-all-start.1 = ((bf16[2,1,8,120,2112]{3,2,0,1,4:T(8,128)(2,1)}), bf16[2,1,8,120,2112]{3,2,0,1,4:T(8,128)(2,1)}, u32[]{:S(2)}, u32[]{:S(2)}) async-start(bf16[2,1,8,120,2112]{3,2,0,1,4:T(8,128)(2,1)} %copy.18), calls=%async_computation.1 | async-start | bytes 17301504 | tf_op jit(solution)/shard_map/all_to_all | solution.py:16
  150.4 0.0 reduce-scatter.7.cloned.1.call-start
  150.4 8.2 %copy.21 = bf16[120,132,256]{2,1,0:T(8,128)(2,1)} copy(bf16[120,132,256]{2,0,1:T(8,128)(2,1)} %param.6) | data formatting | bytes 16220160 | tf_op args[1]
  158.6 11.9 %reshape.16 = bf16[15840,256]{1,0:T(8,128)(2,1)} reshape(bf16[120,132,256]{2,1,0:T(8,128)(2,1)} %copy.21) | data formatting | bytes 16220160 | tf_op jit(solution)/shard_map/reshape | solution.py:32
  170.6 135.1 %all-to-all-done.1 = bf16[2,1,8,120,2112]{3,2,0,1,4:T(8,128)(2,1)} async-done(((bf16[2,1,8,120,2112]{3,2,0,1,4:T(8,128)(2,1)}), bf16[2,1,8,120,2112]{3,2,0,1,4:T(8,128)(2,1)}, u32[]{:S(2)}, u32[]{:S(2)}) %all-to-all-start.1) | async-done | bytes 8110112 | tf_op jit(solution)/shard_map/all_to_all | solution.py:16
  305.7 7.2 %copy.19 = bf16[2,1,8,120,2112]{3,2,4,0,1:T(8,128)(2,1)} copy(bf16[2,1,8,120,2112]{3,2,0,1,4:T(8,128)(2,1)} %all-to-all-done.1) | data formatting | bytes 16220160 | tf_op jit(solution)/shard_map/all_to_all | solution.py:16
  312.8 15.9 %copy.20 = bf16[2,16,1,8,120,132]{5,4,3,1,0,2:T(8,128)(2,1)} copy(bf16[2,16,1,8,120,132]{4,3,5,1,0,2:T(8,128)(2,1)} %bitcast.21) | data formatting | bytes 16220160 | tf_op jit(solution)/shard_map/all_to_all | solution.py:16
  328.7 19.9 %reshape.15 = bf16[256,15840]{1,0:T(8,128)(2,1)} reshape(bf16[2,16,1,8,120,132]{5,4,3,1,0,2:T(8,128)(2,1)} %copy.20) | data formatting | bytes 16220160 | tf_op jit(solution)/shard_map/reshape | solution.py:31
  348.7 7.9 %convolution_bitcast_fusion = f32[256,256]{0,1:T(8,128)S(1)} fusion(bf16[256,15840]{1,0:T(8,128)(2,1)} %reshape.15, bf16[15840,256]{1,0:T(8,128)(2,1)} %reshape.16), kind=kOutput, calls=%fused_computation.4 | convolution fusion | flops 2076180480 | bytes 16482304 | tf_op jit(solution)/shard_map/dot_general | solution.py:34
  356.6 0.8 copy.23
  357.4 0.0 reduce-scatter.7.cloned.1.call-update
  357.4 0.0 reduce-scatter.5.cloned.1.call-start
  357.5 87.3 %reduce-scatter.7.cloned.1.call-done = f32[16,256]{1,0:T(8,128)} async-done(((f32[256,256]{1,0:T(8,128)}), f32[16,256]{1,0:T(8,128)}) %reduce-scatter.7.cloned.1.call-update) | async-done | bytes 16400 | tf_op jit(solution)/shard_map/reduce_scatter | solution.py:33
  444.8 0.0 reduce-scatter.5.cloned.1.call-update
  444.8 11.0 %reduce-scatter.5.cloned.1.call-done = f32[16,128]{1,0:T(8,128)} async-done(((f32[16,256]{1,0:T(8,128)}), f32[16,128]{1,0:T(8,128)}) %reduce-scatter.5.cloned.1.call-update) | async-done | bytes 8208 | tf_op jit(solution)/shard_map/reduce_scatter | solution.py:41
  455.8 1.4 bitcast_divide_fusion
  (4 shorter events, 0.0 us)
Async XLA Ops:
  144.1 161.5 %all-to-all-start.1 = ((bf16[2,1,8,120,2112]{3,2,0,1,4:T(8,128)(2,1)}), bf16[2,1,8,120,2112]{3,2,0,1,4:T(8,128)(2,1)}, u32[]{:S(2)}, u32[]{:S(2)}) async-start(bf16[2,1,8,120,2112]{3,2,0,1,4:T(8,128)(2,1)} %copy.18), calls=%async_computation.1 | async-start | bytes 17301504 | tf_op jit(solution)/shard_map/all_to_all | solution.py:16
  150.4 294.4 %reduce-scatter.7.cloned.1.call-start = ((), (), s32[]{:S(2)}) async-start(), calls=%async_computation.5 | async-start | bytes 278528 | tf_op jit(solution)/shard_map/reduce_scatter | solution.py:33
  348.7 107.2 %copy-start = (f32[16]{0:T(128)S(1)}, f32[16]{0:T(128)}, u32[]{:S(2)}) copy-start(f32[16]{0:T(128)} %param.9) | copy-start | bytes 196
  348.7 107.2 %copy-start.1 = (f32[128]{0:T(128)S(1)}, f32[128]{0:T(128)}, u32[]{:S(2)}) copy-start(f32[128]{0:T(128)} %param.8) | copy-start | bytes 1540
  357.4 98.4 %reduce-scatter.5.cloned.1.call-start = ((), (), s32[]{:S(2)}) async-start(), calls=%async_computation.4 | async-start | bytes 24576 | tf_op jit(solution)/shard_map/reduce_scatter | solution.py:41
Sparse Core Ops, SparseCore 0:
  357.6 87.2 reduce-scatter.6
  447.0 8.7 reduce-scatter.4
